TPU v7x, 128 devices: a whole 4x4x4 slice. The times are simulated.
128 devices in a mesh: rep: 8 (over y, x_lo), row: 16 (over x_hi, z, core).
Axes of the slice: x: 4 (x_hi: 2, x_lo: 2; x = x_hi * 2 + x_lo), y: 4, z: 4, core: 2. Of those that a mesh axis runs over, the one named last changes fastest.
Arguments:
- features: bfloat16 [262144, 128], P(('rep', 'row')), may hold values from -6 to 6
- degrees: int32 [262144], P(('rep', 'row')), may hold values from 4 to 128
- tile_values: bfloat16 [98304, 128, 128], P(('rep', 'row')), may hold values from 0 to 3, as said below
- tile_rows: int32 [98304], P(('rep', 'row')), may hold values from 0 to 127
- tile_cols: int32 [98304], P(('rep', 'row')), may hold values from 0 to 255
- tile_live: int32 [128], P(('rep', 'row')), may hold values from 384 to 768, as said below
- weight: bfloat16 [128, 128], replicated, may hold values from -0.5 to 0.5
- bias: float32 [128], replicated, may hold values from -1 to 1
Outputs:
- activations: bfloat16 [262144, 128], P(('rep', 'row'))
Inputs may be any that keep to these rules, and one draw needn't show every extreme that they name: `tile_live`: at least one device has all 768 slots live. `tile_values`: sparse tiles of small integer edge counts, mostly zeros and ones.
All inputs are finite; a program needn't handle non-finite values.
Results may differ from a plain program's by a relative error of at most 0.0053.
Values may be sent and summed in bfloat16 or wider, within the bound.
A program may use at most 256 MiB of HBM per device.

v0:
```python
import jax
import jax.numpy as jnp
from jax import lax
from jax.sharding import PartitionSpec as P


def per_device(features, degrees, tile_values, tile_rows, tile_cols, tile_live, weight, bias):
    owned = features.shape[0]
    per_block = owned // 128
    groups = lax.axis_size("rep")
    slots_here = tile_values.shape[0]
    width = features.shape[1]
    scale = lax.rsqrt(degrees.astype(jnp.float32))
    scaled = (features.astype(jnp.float32) * scale[:, None]).astype(jnp.bfloat16)
    gathered = lax.all_gather(scaled, "row", axis=0, tiled=True)
    col_tiles = gathered.reshape(-1, 128, width)[tile_cols]
    prods = jnp.einsum("kab,kbf->kaf", tile_values, col_tiles, preferred_element_type=jnp.float32)
    alive = (jnp.arange(slots_here, dtype=jnp.int32) < tile_live[0]).astype(jnp.float32)
    prods = prods * alive[:, None, None]
    partial_value = jax.ops.segment_sum(prods, tile_rows, num_segments=groups * per_block)
    partial_value = partial_value.reshape(groups * owned, width)
    totals = lax.psum(partial_value, "rep")
    own_sum = lax.dynamic_slice_in_dim(totals, lax.axis_index("rep") * owned, owned, 0)
    aggregated = (own_sum * scale[:, None]).astype(jnp.bfloat16)
    mixed = jnp.dot(aggregated, weight, preferred_element_type=jnp.float32) + bias[None, :]
    return jax.nn.relu(mixed).astype(jnp.bfloat16)


def solution(mesh):
    return jax.shard_map(
        per_device,
        mesh=mesh,
        in_specs=(
            P(("rep", "row"), None),
            P(("rep", "row")),
            P(("rep", "row"), None, None),
            P(("rep", "row")),
            P(("rep", "row")),
            P(("rep", "row")),
            P(),
            P(),
        ),
        out_specs=P(("rep", "row"), None),
        check_vma=False,
    )
```

profile of v0, /device:TPU:0, one launch (start us, length us, event | category | flops | bytes accessed | tf_op | source)
XLA Modules:
  0.0 703.3 jit_solution(4155334828526962372)
XLA Ops:
  6.5 0.0 copy-start
  6.5 0.0 all-gather.2.cloned.1.call-start
  6.5 0.7 convert_rsqrt_fusion
  7.3 2.2 multiply_convert_fusion.1
  9.4 0.0 all-gather.2.cloned.1.call-update
  9.5 0.0 all-reduce.2.cloned.1.call-start
  10.1 0.7 compare_select_fusion
  10.9 74.6 %all-gather.2.cloned.1.call-done = bf16[32768,128]{1,0:T(8,128)(2,1)} async-done(((bf16[2048,128]{1,0:T(8,128)(2,1)}), bf16[32768,128]{1,0:T(8,128)(2,1)}) %all-gather.2.cloned.1.call-update) | async-done | bytes 8388624 | tf_op jit(solution)/shard_map/all_gather | solution.py:15
  85.5 22.6 %gather_fusion = bf16[768,128,128]{2,1,0:T(8,128)(2,1)} fusion(bf16[256,128,128]{2,1,0:T(8,128)(2,1)} %bitcast.10, s32[1024]{0:T(1024)S(1)} %pad_clamp_fusion), kind=kCustom, calls=%fused_computation | custom fusion | bytes 50334720 | tf_op jit(solution)/shard_map/gather | solution.py:16
  108.0 40.7 %multiply_bitcast_fusion = f32[768,128,128]{1,2,0:T(8,128)} fusion(f32[768]{0:T(1024)S(1)} %fusion.3, bf16[768,128,128]{2,1,0:T(8,128)(2,1)} %gather_fusion, bf16[768,128,128]{2,1,0:T(8,128)(2,1)} %param.10), kind=kOutput, calls=%fused_computation.2 | convolution fusion | flops 3233808384 | bytes 100666368 | tf_op jit(solution)/shard_map/kab,kbf->kaf/dot_general | solution.py:17
  148.8 0.0 copy-start.1
  148.8 48.8 %copy.11 = f32[768,128,128]{2,1,0:T(8,128)} copy(f32[768,128,128]{1,2,0:T(8,128)} %multiply_bitcast_fusion) | data formatting | bytes 100663296 | tf_op jit(solution)/shard_map/mul | solution.py:19
  197.6 4.3 broadcast_in_dim.6
  201.8 0.0 copy-done.1
  201.8 0.0 copy-start.2
  201.8 154.2 %scatter_fusion = f32[128,128,128]{2,1,0:T(8,128)} fusion(f32[128,128,128]{2,1,0:T(8,128)} %broadcast_in_dim.6, s32[768]{0:T(1024)S(1)} %copy-done.1, f32[768,128,128]{2,1,0:T(8,128)} %copy.11), kind=kCustom, calls=%fused_computation.1 | custom fusion | flops 12582912 | bytes 150998016 | tf_op jit(solution)/shard_map/scatter-add | solution.py:20
  356.1 0.0 all-reduce.2.cloned.1.call-update
  356.1 337.8 %all-reduce.2.cloned.1.call-done = f32[16384,128]{1,0:T(8,128)} async-done(((f32[16384,128]{1,0:T(8,128)}), f32[16384,128]{1,0:T(8,128)}) %all-reduce.2.cloned.1.call-update) | async-done | bytes 8388624 | tf_op jit(solution)/shard_map/psum | solution.py:22
  693.9 0.0 copy-done
  694.0 0.0 copy-done.2
  694.0 2.5 fusion.1
  (2 shorter events, 0.0 us)
Async XLA Ops:
  6.5 687.4 %copy-start = (bf16[128,128]{1,0:T(8,128)(2,1)S(1)}, bf16[128,128]{1,0:T(8,128)(2,1)}, u32[]{:S(2)}) copy-start(bf16[128,128]{1,0:T(8,128)(2,1)} %param.14) | copy-start | bytes 98308
  6.5 78.9 %all-gather.2.cloned.1.call-start = ((), (), s32[]{:S(2)}) async-start(), calls=%async_computation | async-start | bytes 8912896 | tf_op jit(solution)/shard_map/all_gather | solution.py:15
  9.5 684.5 %all-reduce.2.cloned.1.call-start = ((), (), s32[]{:S(2)}) async-start(), calls=%async_computation.1 | async-start | bytes 16777216 | tf_op jit(solution)/shard_map/psum | solution.py:22
  148.8 53.1 %copy-start.1 = (s32[768]{0:T(1024)S(1)}, s32[768]{0:T(1024)}, u32[]{:S(2)}) copy-start(s32[768]{0:T(1024)} %param.11) | copy-start | bytes 9220
  201.8 492.1 %copy-start.2 = (f32[128]{0:T(128)S(1)}, f32[128]{0:T(128)}, u32[]{:S(2)}) copy-start(f32[128]{0:T(128)} %param.15) | copy-start | bytes 1540
Sparse Core Ops, SparseCore 0:
  9.8 75.5 all-gather.1
  356.2 337.6 all-reduce.1
where the time goes:
time: 706 us; the launch traced here: 703 us
  waiting for transfers between devices  412 us (58%)
  other arithmetic  158 us (22%)
  local copies, waits for them, and re-layouts  75.7 us (11%)
  matrix products  43.2 us (6%)
  between operations  14.1 us (2%)
    psum x1, waiting for transfers between devices, per_device(): totals = lax.psum(partial_value, 'rep')  338 us
    scatter-add x1, other arithmetic, per_device(): jax.ops.segment_sum(prods, tile_rows, num_segments=groups * per_block)  154 us
    all_gather x1, waiting for transfers between devices, per_device(): gathered = lax.all_gather(scaled, 'row', axis=0, tiled=True)  74.6 us
    mul x1, local copies, waits for them, and re-layouts, per_device(): prods = prods * alive[:, None, None]  48.8 us
    dot_general x1, matrix products, per_device(): jnp.einsum('kab,kbf->kaf', tile_values, col_tiles, preferred_element_type...  40.7 us
    gather x1, local copies, waits for them, and re-layouts, per_device(): col_tiles = gathered.reshape(-1, 128, width)[tile_cols]  22.6 us
  transfers between devices with their start and end apart: 2, of which 2 were waited for; matrix products, arithmetic and copies ran while one was open for 0% of the time, Pallas kernels for 0%

commit v1 on v0

v1 whole, which is shorter than its diff:
```python
import functools

import jax
import jax.numpy as jnp
from jax import lax
from jax.experimental import pallas as pl
from jax.experimental.pallas import tpu as pltpu
from jax.sharding import PartitionSpec as P

MESH = pl.DeviceIdType.MESH
F32, BF16, I32 = jnp.float32, jnp.bfloat16, jnp.int32
NT = (((1,), (1,)), ((), ()))
TN = (((0,), (0,)), ((), ()))

T = 128
CH = 2
FC = 128 // CH
SLOTS = 768
STEPS = 448
UNROLL = 32
ITERS = STEPS // UNROLL
NX = 2
NA = 6
NB = 16 - NA
HA, HB = NA // 2, NB // 2
ROW_KEEP, ROW_END = 8, 12


def make_plan(rows_ref, cols_ref, live, plan_ref):
    lane = lax.broadcasted_iota(I32, (T, T), 1)
    sub = lax.broadcasted_iota(I32, (T, T), 0)
    before = (sub < lane).astype(BF16)
    lane1 = lax.broadcasted_iota(I32, (1, T), 1)
    lane_f = lane.astype(F32)
    zero = jnp.zeros((T, T), F32)
    carry = jnp.zeros((T, 1), F32)
    hots, ranks, alive = [], [], []
    for j in range(SLOTS // T):
        there = (lane1 + j * T) < live
        r = jnp.where(there, rows_ref[j : j + 1, :], T)
        hot = jnp.where(sub == r, 1.0, 0.0).astype(F32)
        earlier = jnp.dot(hot.astype(BF16), before, preferred_element_type=F32)
        ranks.append(jnp.sum(hot * (earlier + carry), axis=0, keepdims=True))
        carry = carry + jnp.sum(hot, axis=1, keepdims=True)
        hots.append(hot)
        alive.append(there)
    pairs = jnp.broadcast_to(jnp.floor((carry + 1.0) * 0.5), (T, T))
    start = jnp.sum(jnp.where(lane < sub, pairs.T, zero), axis=1, keepdims=True)
    start = jnp.broadcast_to(start, (T, T))
    places, codes = [], []
    for j in range(SLOTS // T):
        place = ranks[j] + 2.0 * jnp.sum(hots[j] * start, axis=0, keepdims=True)
        places.append(jnp.where(alive[j], place, -1.0))
        codes.append(((lane1 + (j * T - SLOTS)) * 256 + cols_ref[j : j + 1, :]).astype(F32))
    fill = [jnp.full((2, T), -1.0, F32)]
    places_t = jnp.concatenate(places + fill, axis=0).T
    codes_t = jnp.concatenate(codes + fill, axis=0).T
    sums = [zero] * (2 * STEPS // T)
    for j in range(SLOTS // T):
        place = jnp.broadcast_to(places_t[:, j : j + 1], (T, T))
        code = jnp.broadcast_to(codes_t[:, j : j + 1], (T, T))
        for b in range(2 * STEPS // T):
            sums[b] = sums[b] + jnp.where(place == lane_f + float(b * T), code, zero)
    for b in range(2 * STEPS // T):
        code = jnp.sum(sums[b], axis=0, keepdims=True).astype(I32) + SLOTS * 256
        plan_ref[b : b + 1, :] = jnp.clip(code, 0, SLOTS * 256 + 255)
    for b in range(4):
        begins = jnp.where((start == lane_f + float(b * T)) & (pairs > 0.0), 1.0, 0.0)
        plan_ref[ROW_KEEP + b : ROW_KEEP + b + 1, :] = 1 - jnp.sum(begins, axis=0, keepdims=True).astype(I32)
    ends = jnp.where(pairs > 0.0, start + pairs - 1.0, float(STEPS))
    plan_ref[ROW_END : ROW_END + 1, :] = jnp.clip(ends.T[0:1, :].astype(I32), 0, STEPS)


def kernel(
    feat_ref, deg_ref, tiles_ref, rows_ref, cols_ref, live_ref, weight_ref, bias_ref, out_ref,
    a_buf, x0, x1, s_buf, o0, o1, plan_v, plan_s, agg,
    rxa, rb1l, rb1h, rbm, rbp, ra1l, ra1h, ram, rap, sxb, rxb,
    a_sem, p_sem, gs, gr, rs, rr,
):
    rep, row = lax.axis_index("rep"), lax.axis_index("row")
    y, l = rep // 2, rep % 2
    h, z, c = row // 8, (row // 2) % 4, row % 2
    zp = (rep, h * 8 + ((z + 1) % 4) * 2 + c)
    zm = (rep, h * 8 + ((z + 3) % 4) * 2 + c)
    xh = (rep, (1 - h) * 8 + z * 2 + c)
    sib = (rep, h * 8 + z * 2 + (1 - c))
    xl = (y * 2 + (1 - l), row)
    yp = (((y + 1) % 4) * 2 + l, row)
    ym = (((y + 3) % 4) * 2 + l, row)
    partners = (zp, zm, xh, sib, xl, yp, ym)
    xs, outs = (x0, x1), (o0, o1)

    loads = []
    per = SLOTS // 6
    for j in range(6):
        load = pltpu.make_async_copy(
            tiles_ref.at[pl.ds(j * per, per)], a_buf.at[pl.ds(j * per, per)], a_sem.at[j]
        )
        load.start()
        loads.append(load)
    barrier = pltpu.get_barrier_semaphore()
    for device in partners:
        pl.semaphore_signal(barrier, inc=1, device_id=device, device_id_type=MESH)

    scale = lax.rsqrt(deg_ref[...].astype(F32))
    for t in range(16):
        turned = feat_ref[t * T : (t + 1) * T, :].T.astype(F32)
        scaled = (turned * scale[t : t + 1, :]).astype(BF16)
        for ch in range(CH):
            xs[ch][row * 16 + t] = scaled[ch * FC : (ch + 1) * FC, :]
    a_buf[SLOTS] = jnp.zeros((T, T), BF16)
    s_buf[STEPS] = jnp.zeros((FC, T), BF16)

    pl.semaphore_wait(barrier, len(partners))

    def block(dh, dz, core=None):
        return ((h + dh) % 2) * 8 + ((z + dz) % 4) * 2 + (c if core is None else core)

    def g_copy(ch, k, to, blk, lo=0, hi=16):
        ref = xs[ch].at[pl.ds(blk * 16 + lo, hi - lo)]
        return pltpu.make_async_remote_copy(
            ref, ref, gs.at[ch, k], gr.at[ch, k], device_id=to, device_id_type=MESH
        )

    other = 1 - c
    G = {
        0: (zp, (0, 0), (0, 3), 0, 16),
        1: (zm, (0, 0), (0, 1), 0, 16),
        2: (xh, (0, 0), (1, 0), 0, 16),
        3: (sib, (0, 0), None, 0, 16),
        4: (zp, (0, 3), (0, 2), 0, 8),
        5: (sib, (0, 3), None, 0, 16),
        6: (zm, (0, 1), (0, 2), 8, 16),
        7: (sib, (0, 1), None, 0, 16),
        8: (zp, (1, 0), (1, 3), NX, 16),
        9: (zm, (1, 0), (1, 1), NX, 16),
        10: (sib, (1, 0), None, 0, 16),
        11: (xh, (0, 2), (1, 2), 0, 8),
        12: (xh, (0, 2), (1, 2), 8, 16),
        13: (sib, (0, 2), None, 0, 8),
        14: (sib, (0, 2), None, 8, 16),
        15: (sib, (1, 3), None, NX, 16),
        16: (sib, (1, 1), None, NX, 16),
        17: (sib, (1, 2), None, 0, 8),
        18: (sib, (1, 2), None, 8, 16),
        19: (xh, (0, 3), (1, 3), 0, NX),
        20: (xh, (0, 1), (1, 1), 0, NX),
        21: (sib, (1, 3), None, 0, NX),
        22: (sib, (1, 1), None, 0, NX),
    }

    def g_send(ch, *ks):
        for k in ks:
            to, sent, _, lo, hi = G[k]
            g_copy(ch, k, to, block(*sent), lo, hi).start()

    def g_recv(ch, *ks):
        for k in ks:
            to, sent, got, lo, hi = G[k]
            blk = block(*sent, core=other) if got is None else block(*got)
            g_copy(ch, k, to, blk, lo, hi).wait_recv()

    def g_flush(ch):
        for k, (to, sent, _, lo, hi) in G.items():
            g_copy(ch, k, to, block(*sent), lo, hi).wait_send()

    def g_first(ch):
        g_send(ch, 0, 1, 2, 3)

    def g_second(ch):
        g_recv(ch, 0)
        g_send(ch, 4, 19, 5)
        g_recv(ch, 1)
        g_send(ch, 6, 20, 7)
        g_recv(ch, 2)
        g_send(ch, 8, 9, 10)

    def g_third(ch):
        g_recv(ch, 4)
        g_send(ch, 11, 13)
        g_recv(ch, 6)
        g_send(ch, 12, 14)

    def g_fourth(ch):
        g_recv(ch, 19)
        g_send(ch, 21)
        g_recv(ch, 20)
        g_send(ch, 22)
        g_recv(ch, 8)
        g_send(ch, 15)
        g_recv(ch, 9)
        g_send(ch, 16)

    def g_last(ch):
        g_recv(ch, 11)
        g_send(ch, 17)
        g_recv(ch, 12)
        g_send(ch, 18)
        g_recv(ch, 3, 5, 7, 10, 13, 14, 15, 16, 21, 22, 17, 18)

    def at_y(d):
        return (y + d) % 4

    alo, ahi = pl.ds(0, HA), pl.ds(HA, HA)
    blo, bhi = pl.ds(NA, HB), pl.ds(NA + HB, HB)
    zlo, zhi = pl.ds(0, HB), pl.ds(HB, HB)

    def r_copy(ch, k):
        o = outs[ch]
        if k < 4:
            src, dst, to = o.at[at_y(k) * 2 + (1 - l), pl.ds(0, NA)], rxa.at[ch, k], xl
        elif k < 10:
            where, part, dst, to = {
                4: (at_y(2), blo, rb1l.at[ch], ym),
                5: (at_y(2), bhi, rb1h.at[ch], yp),
                6: (at_y(1), blo, rbm.at[ch, :, zlo], yp),
                7: (at_y(3), bhi, rbp.at[ch, :, zhi], ym),
                8: (at_y(3), blo, rbp.at[ch, :, zlo], ym),
                9: (at_y(1), bhi, rbm.at[ch, :, zhi], yp),
            }[k]
            src = o.at[pl.ds(where * 2, 2), part]
        elif k < 16:
            where, part, dst, to = {
                10: (at_y(2), alo, ra1l.at[ch], ym),
                11: (at_y(2), ahi, ra1h.at[ch], yp),
                12: (at_y(1), alo, ram.at[ch, alo], yp),
                13: (at_y(3), ahi, rap.at[ch, ahi], ym),
                14: (at_y(3), alo, rap.at[ch, alo], ym),
                15: (at_y(1), ahi, ram.at[ch, ahi], yp),
            }[k]
            src = o.at[where * 2 + l, part]
        else:
            src, dst, to = sxb.at[ch], rxb.at[ch], xl
        return pltpu.make_async_remote_copy(
            src, dst, rs.at[ch, k], rr.at[ch, k], device_id=to, device_id_type=MESH
        )

    def r_send(ch, *ks):
        for k in ks:
            r_copy(ch, k).start()

    def r_recv(ch, *ks):
        for k in ks:
            r_copy(ch, k).wait_recv()

    def add_to(ch, part, at, count, got):
        o = outs[ch]

        def body(t, _):
            o[part, at + t] = (o[part, at + t].astype(F32) + got(t).astype(F32)).astype(BF16)
            return 0

        lax.fori_loop(0, count, body, 0)

    def r_first(ch):
        r_send(ch, 4, 5, 2, 6, 7, 1, 3, 0)

    def r_second(ch):
        r_recv(ch, 4)
        for side in range(2):
            add_to(ch, at_y(3) * 2 + side, NA, HB, lambda t: rb1l[ch, side, t])
        r_send(ch, 8)
        r_recv(ch, 5)
        for side in range(2):
            add_to(ch, at_y(1) * 2 + side, NA + HB, HB, lambda t: rb1h[ch, side, t])
        r_send(ch, 9)
        r_recv(ch, 2)
        add_to(ch, at_y(2) * 2 + l, 0, NA, lambda t: rxa[ch, 2, t])
        r_send(ch, 10, 11)

    def r_third(ch):
        r_recv(ch, 1)
        add_to(ch, at_y(1) * 2 + l, 0, NA, lambda t: rxa[ch, 1, t])
        r_send(ch, 12)
        r_recv(ch, 3)
        add_to(ch, at_y(3) * 2 + l, 0, NA, lambda t: rxa[ch, 3, t])
        r_send(ch, 13)

    def r_fourth(ch):
        r_recv(ch, 6, 7, 8, 9)

        def body(t, _):
            total = outs[ch][y * 2 + (1 - l), NA + t].astype(F32)
            total = total + rbm[ch, 1 - l, t].astype(F32) + rbp[ch, 1 - l, t].astype(F32)
            sxb[ch, t] = total.astype(BF16)
            return 0

        lax.fori_loop(0, NB, body, 0)
        r_send(ch, 16)

    def r_fifth(ch):
        r_recv(ch, 10)
        add_to(ch, at_y(3) * 2 + l, 0, HA, lambda t: ra1l[ch, t])
        r_send(ch, 14)
        r_recv(ch, 11)
        add_to(ch, at_y(1) * 2 + l, HA, HA, lambda t: ra1h[ch, t])
        r_send(ch, 15)

    def finish(ch, t, total):
        agg[t, ch * FC : (ch + 1) * FC, :] = (total * lax.rsqrt(deg_ref[pl.ds(t, 1), :].astype(F32))).astype(BF16)

    def r_last(ch):
        r_recv(ch, 0, 12, 13, 14, 15)

        def body_a(t, _):
            total = outs[ch][y * 2 + l, t].astype(F32) + rxa[ch, 0, t].astype(F32)
            finish(ch, t, total + ram[ch, t].astype(F32) + rap[ch, t].astype(F32))
            return 0

        lax.fori_loop(0, NA, body_a, 0)
        r_recv(ch, 16)

        def body_b(t, _):
            total = outs[ch][y * 2 + l, NA + t].astype(F32) + rxb[ch, t].astype(F32)
            finish(ch, NA + t, total + rbm[ch, l, t].astype(F32) + rbp[ch, l, t].astype(F32))
            return 0

        lax.fori_loop(0, NB, body_b, 0)

    def products(ch, events):
        x = xs[ch]

        def body(i, acc):
            for at, act in events:
                pl.when(i == at)(act)
            for u in range(UNROLL):
                spot = (i % 2) * (2 * UNROLL) + 2 * u
                first = jnp.clip(plan_s[i // 2, spot], 0, SLOTS * 256 + 255)
                second = jnp.clip(plan_s[i // 2, spot + 1], 0, SLOTS * 256 + 255)
                keep = plan_s[ROW_KEEP + i // 4, (i % 4) * UNROLL + u].astype(F32)
                values = jnp.concatenate([a_buf[first >> 8], a_buf[second >> 8]], axis=1)
                nodes = jnp.concatenate([x[first & 255], x[second & 255]], axis=1)
                acc = acc * keep + lax.dot_general(nodes, values, NT, preferred_element_type=F32)
                s_buf[i * UNROLL + u] = acc.astype(BF16)
            return acc

        lax.fori_loop(0, ITERS, body, jnp.zeros((FC, T), F32))

    def extract(ch):
        o = outs[ch]

        def body(i, _):
            for u in range(16):
                o[i, u] = s_buf[jnp.clip(plan_s[ROW_END, i * 16 + u], 0, STEPS)]
            return 0

        lax.fori_loop(0, 8, body, 0)

    g_first(0)
    make_plan(rows_ref, cols_ref, live_ref[0], plan_v)
    to_smem = pltpu.make_async_copy(plan_v, plan_s, p_sem)
    to_smem.start()
    g_second(0)
    g_third(0)
    g_first(1)
    g_fourth(0)
    to_smem.wait()
    for load in loads:
        load.wait()
    g_last(0)

    products(0, [(6, lambda: g_second(1)), (9, lambda: g_third(1)), (12, lambda: g_fourth(1))])
    extract(0)
    r_first(0)
    g_last(1)
    products(
        1,
        [
            (4, lambda: r_second(0)),
            (7, lambda: r_third(0)),
            (9, lambda: r_fourth(0)),
            (11, lambda: r_fifth(0)),
        ],
    )
    extract(1)
    r_first(1)
    r_last(0)
    r_second(1)
    r_third(1)
    r_fourth(1)
    r_fifth(1)
    r_last(1)

    def body(t, _):
        mixed = lax.dot_general(agg[t], weight_ref[...], TN, preferred_element_type=F32)
        out_ref[pl.ds(t * T, T), :] = jnp.maximum(mixed + bias_ref[...], 0.0).astype(BF16)
        return 0

    lax.fori_loop(0, 16, body, 0)
    for ch in range(CH):
        g_flush(ch)
        for k in range(17):
            r_copy(ch, k).wait_send()


def per_device(features, degrees, tile_values, tile_rows, tile_cols, tile_live, weight, bias):
    vmem = pl.BlockSpec(memory_space=pltpu.VMEM)
    tile = (FC, T)
    return pl.pallas_call(
        kernel,
        out_shape=jax.ShapeDtypeStruct(features.shape, BF16),
        in_specs=[
            vmem, vmem, pl.BlockSpec(memory_space=pl.ANY), vmem, vmem,
            pl.BlockSpec(memory_space=pltpu.SMEM), vmem, vmem,
        ],
        out_specs=vmem,
        scratch_shapes=[
            pltpu.VMEM((SLOTS + 1, T, T), BF16),
            pltpu.VMEM((256,) + tile, BF16),
            pltpu.VMEM((256,) + tile, BF16),
            pltpu.VMEM((STEPS + 1,) + tile, BF16),
            pltpu.VMEM((8, 16) + tile, BF16),
            pltpu.VMEM((8, 16) + tile, BF16),
            pltpu.VMEM((16, T), I32),
            pltpu.SMEM((16, T), I32),
            pltpu.VMEM((16, 128, T), BF16),
            pltpu.VMEM((CH, 4, NA) + tile, BF16),
            pltpu.VMEM((CH, 2, HB) + tile, BF16),
            pltpu.VMEM((CH, 2, HB) + tile, BF16),
            pltpu.VMEM((CH, 2, NB) + tile, BF16),
            pltpu.VMEM((CH, 2, NB) + tile, BF16),
            pltpu.VMEM((CH, HA) + tile, BF16),
            pltpu.VMEM((CH, HA) + tile, BF16),
            pltpu.VMEM((CH, NA) + tile, BF16),
            pltpu.VMEM((CH, NA) + tile, BF16),
            pltpu.VMEM((CH, NB) + tile, BF16),
            pltpu.VMEM((CH, NB) + tile, BF16),
            pltpu.SemaphoreType.DMA((6,)),
            pltpu.SemaphoreType.DMA,
            pltpu.SemaphoreType.DMA((CH, 23)),
            pltpu.SemaphoreType.DMA((CH, 23)),
            pltpu.SemaphoreType.DMA((CH, 17)),
            pltpu.SemaphoreType.DMA((CH, 17)),
        ],
        compiler_params=pltpu.CompilerParams(
            collective_id=0, has_side_effects=True, vmem_limit_bytes=60 << 20
        ),
        name="graph_layer",
    )(
        features,
        degrees.reshape(16, T),
        tile_values,
        tile_rows.reshape(SLOTS // T, T),
        tile_cols.reshape(SLOTS // T, T),
        tile_live,
        weight,
        bias.reshape(1, 128),
    )


def solution(mesh):
    return jax.shard_map(
        per_device,
        mesh=mesh,
        in_specs=(
            P(("rep", "row"), None),
            P(("rep", "row")),
            P(("rep", "row"), None, None),
            P(("rep", "row")),
            P(("rep", "row")),
            P(("rep", "row")),
            P(),
            P(),
        ),
        out_specs=P(("rep", "row"), None),
        check_vma=False,
    )
```

time: 706 us -> 91.4 us (0.13)
  waiting for transfers between devices: 412 us -> 0 us
  other arithmetic: 158 us -> 0 us
  Pallas kernels: 0 us -> 88.7 us
  local copies, waits for them, and re-layouts: 75.7 us -> 1.87 us
  matrix products: 43.2 us -> 0 us
  between operations: 14.1 us -> 0.66 us
    psum x1 -> x0, waiting for transfers between devices: 338 us -> none  [per_device(): totals = lax.psum(partial_value, 'rep')]
    scatter-add x1 -> x0, other arithmetic: 154 us -> none  [per_device(): jax.ops.segment_sum(prods, tile_rows, num_segments=groups * per_block)]
    pallas_call x0 -> x1, Pallas kernels: none -> 88.7 us  [per_device(): pl.pallas_call(kernel, out_shape=jax.ShapeDtypeStruct(features.shape, BF1...]
    all_gather x1 -> x0, waiting for transfers between devices: 74.6 us -> none  [per_device(): gathered = lax.all_gather(scaled, 'row', axis=0, tiled=True)]
    mul x1 -> x0, local copies, waits for them, and re-layouts: 48.8 us -> none  [per_device(): prods = prods * alive[:, None, None]]
    dot_general x2 -> x0, matrix products: 43.2 us -> none  [the longest x1 40.7 us: per_device(): jnp.einsum('kab,kbf->kaf', tile_values, col_tiles, preferred_element_type...]
    gather x1 -> x0, local copies, waits for them, and re-layouts: 22.6 us -> none  [per_device(): col_tiles = gathered.reshape(-1, 128, width)[tile_cols]]
  transfers between devices with their start and end apart: 2 -> 0, of which waited for: 2 -> 0; matrix products, arithmetic and copies ran while one was open for 0% -> 0% of each run, Pallas kernels for 0% -> 0%
where the time goes in v1:
time: 91.4 us; the launch traced here: 91.2 us
  Pallas kernels  88.7 us (97%)
  local copies, waits for them, and re-layouts  1.87 us (2%)
    pallas_call x1, Pallas kernels, per_device(): pl.pallas_call(kernel, out_shape=jax.ShapeDtypeStruct(features.shape, BF1...  88.7 us
    unnamed x1, local copies, waits for them, and re-layouts  1.87 us

profile of v1, /device:TPU:0, one launch (start us, length us, event | category | flops | bytes accessed | tf_op | source)
XLA Modules:
  0.0 91.2 jit_solution(2999423669326551596)
XLA Ops:
  0.7 88.7 %graph_layer.1 = bf16[2048,128]{1,0:T(8,128)(2,1)} custom-call(bf16[2048,128]{1,0:T(8,128)(2,1)} %feat_ref.1, s32[16,128]{1,0:T(8,128)} %bitcast.4, bf16[768,128,128]{2,1,0:T(8,128)(2,1)} %tiles_ref.1, s32[6,128]{1,0:T(8,128)} %bitcast.5, s32[6,128]{1,0:T(8,128)} %bitcast.6, s32[1]{0:T(128)S(6)} %copy.10.live_ref, bf16[128,128]{1,0:T(8,128)(2,1)} %weight_ref.1, ...), custom_call_target="tpu_custom_call" | custom-call | tf_op jit(solution)/shard_map/graph_layer/pallas_call | solution.py:399
  89.3 1.9 %copy.11 = bf16[2048,128]{1,0:T(8,128)(2,1)} copy(bf16[2048,128]{1,0:T(8,128)(2,1)} %graph_layer.1) | data formatting | bytes 1048576

commit v2 on v1

v2 whole, which is shorter than its diff:
```python
import functools

import jax
import jax.numpy as jnp
from jax import lax
from jax.experimental import pallas as pl
from jax.experimental.pallas import tpu as pltpu
from jax.sharding import PartitionSpec as P

MESH = pl.DeviceIdType.MESH
F32, BF16, I32 = jnp.float32, jnp.bfloat16, jnp.int32
NT = (((1,), (1,)), ((), ()))
TN = (((0,), (0,)), ((), ()))

T = 128
CH = 2
FCS = (64, 64)
FOF = (0, FCS[0])
SLOTS = 768
STEPS = 448
UNROLL = 32
ITERS = STEPS // UNROLL
NX = 6
NQ = 4
NA = 6
NB = 16 - NA
HA, HB = NA // 2, NB // 2
ROW_KEEP, ROW_END = 8, 12


def make_plan(rows_ref, cols_ref, live, plan_ref):
    lane = lax.broadcasted_iota(I32, (T, T), 1)
    sub = lax.broadcasted_iota(I32, (T, T), 0)
    before = (sub < lane).astype(BF16)
    lane1 = lax.broadcasted_iota(I32, (1, T), 1)
    lane_f = lane.astype(F32)
    zero = jnp.zeros((T, T), F32)
    carry = jnp.zeros((T, 1), F32)
    hots, ranks, alive = [], [], []
    for j in range(SLOTS // T):
        there = (lane1 + j * T) < live
        r = jnp.where(there, rows_ref[j : j + 1, :], T)
        hot = jnp.where(sub == r, 1.0, 0.0).astype(F32)
        earlier = jnp.dot(hot.astype(BF16), before, preferred_element_type=F32)
        ranks.append(jnp.sum(hot * (earlier + carry), axis=0, keepdims=True))
        carry = carry + jnp.sum(hot, axis=1, keepdims=True)
        hots.append(hot)
        alive.append(there)
    pairs = jnp.broadcast_to(jnp.floor((carry + 1.0) * 0.5), (T, T))
    start = jnp.sum(jnp.where(lane < sub, pairs.T, zero), axis=1, keepdims=True)
    start = jnp.broadcast_to(start, (T, T))
    places, codes = [], []
    for j in range(SLOTS // T):
        place = ranks[j] + 2.0 * jnp.sum(hots[j] * start, axis=0, keepdims=True)
        places.append(jnp.where(alive[j], place, -1.0))
        codes.append(((lane1 + (j * T - SLOTS)) * 256 + cols_ref[j : j + 1, :]).astype(F32))
    fill = [jnp.full((2, T), -1.0, F32)]
    places_t = jnp.concatenate(places + fill, axis=0).T
    codes_t = jnp.concatenate(codes + fill, axis=0).T
    sums = [zero] * (2 * STEPS // T)
    for j in range(SLOTS // T):
        place = jnp.broadcast_to(places_t[:, j : j + 1], (T, T))
        code = jnp.broadcast_to(codes_t[:, j : j + 1], (T, T))
        for b in range(2 * STEPS // T):
            sums[b] = sums[b] + jnp.where(place == lane_f + float(b * T), code, zero)
    for b in range(2 * STEPS // T):
        code = jnp.sum(sums[b], axis=0, keepdims=True).astype(I32) + SLOTS * 256
        plan_ref[b : b + 1, :] = jnp.clip(code, 0, SLOTS * 256 + 255)
    for b in range(4):
        begins = jnp.where((start == lane_f + float(b * T)) & (pairs > 0.0), 1.0, 0.0)
        plan_ref[ROW_KEEP + b : ROW_KEEP + b + 1, :] = 1 - jnp.sum(begins, axis=0, keepdims=True).astype(I32)
    ends = jnp.where(pairs > 0.0, start + pairs - 1.0, float(STEPS))
    plan_ref[ROW_END : ROW_END + 1, :] = jnp.clip(ends.T[0:1, :].astype(I32), 0, STEPS)


def kernel(
    feat_ref, deg_ref, tiles_ref, rows_ref, cols_ref, live_ref, weight_ref, bias_ref, out_ref,
    a_buf, x0, x1, s_buf, o0, o1, plan_v, plan_s, agg,
    *rest,
):
    bufs, (a_sem, p_sem, gs, gr, rs, rr) = rest[:-6], rest[-6:]
    rxa, rb1l, rb1h, rbm, rbp, ra1l, ra1h, ram, rap, sxb, rxb = zip(bufs[:11], bufs[11:])
    rep, row = lax.axis_index("rep"), lax.axis_index("row")
    y, l = rep // 2, rep % 2
    h, z, c = row // 8, (row // 2) % 4, row % 2
    zp = (rep, h * 8 + ((z + 1) % 4) * 2 + c)
    zm = (rep, h * 8 + ((z + 3) % 4) * 2 + c)
    xh = (rep, (1 - h) * 8 + z * 2 + c)
    sib = (rep, h * 8 + z * 2 + (1 - c))
    xl = (y * 2 + (1 - l), row)
    yp = (((y + 1) % 4) * 2 + l, row)
    ym = (((y + 3) % 4) * 2 + l, row)
    partners = (zp, zm, xh, sib, xl, yp, ym)
    xs, outs = (x0, x1), (o0, o1)

    loads = []
    per = SLOTS // 6
    for j in range(6):
        load = pltpu.make_async_copy(
            tiles_ref.at[pl.ds(j * per, per)], a_buf.at[pl.ds(j * per, per)], a_sem.at[j]
        )
        load.start()
        loads.append(load)
    barrier = pltpu.get_barrier_semaphore()
    for device in partners:
        pl.semaphore_signal(barrier, inc=1, device_id=device, device_id_type=MESH)

    scale = lax.rsqrt(deg_ref[...].astype(F32))
    for t in range(16):
        turned = feat_ref[t * T : (t + 1) * T, :].T.astype(F32)
        scaled = (turned * scale[t : t + 1, :]).astype(BF16)
        for ch in range(CH):
            xs[ch][row * 16 + t] = scaled[FOF[ch] : FOF[ch] + FCS[ch], :]
    a_buf[SLOTS] = jnp.zeros((T, T), BF16)
    s_buf[STEPS] = jnp.zeros((max(FCS), T), BF16)

    pl.semaphore_wait(barrier, len(partners))

    def block(dh, dz, core=None):
        return ((h + dh) % 2) * 8 + ((z + dz) % 4) * 2 + (c if core is None else core)

    def g_copy(ch, k, to, blk, lo=0, hi=16):
        ref = xs[ch].at[pl.ds(blk * 16 + lo, hi - lo)]
        return pltpu.make_async_remote_copy(
            ref, ref, gs.at[ch, k], gr.at[ch, k], device_id=to, device_id_type=MESH
        )

    other = 1 - c
    G = {
        0: (zp, (0, 0), (0, 3), 0, 8),
        1: (zm, (0, 0), (0, 1), 8, 16),
        2: (xh, (0, 0), (1, 0), 0, 16),
        3: (sib, (0, 0), None, 0, 16),
        4: (zp, (0, 3), (0, 2), 0, 8),
        5: (sib, (0, 3), None, 0, 16),
        6: (zm, (0, 1), (0, 2), 8, 16),
        7: (sib, (0, 1), None, 0, 16),
        8: (zp, (1, 0), (1, 3), NX, 16),
        9: (zm, (1, 0), (1, 1), 0, 16 - NX),
        10: (sib, (1, 0), None, 0, 16),
        11: (xh, (0, 2), (1, 2), NQ, 8),
        12: (xh, (0, 2), (1, 2), 8, 16 - NQ),
        13: (sib, (0, 2), None, 0, 8),
        14: (sib, (0, 2), None, 8, 16),
        15: (sib, (1, 3), None, NX, 16),
        16: (sib, (1, 1), None, 0, 16 - NX),
        17: (sib, (1, 2), None, NQ, 8),
        18: (sib, (1, 2), None, 8, 16 - NQ),
        19: (xh, (0, 3), (1, 3), 0, NX),
        20: (xh, (0, 1), (1, 1), 16 - NX, 16),
        21: (sib, (1, 3), None, 0, NX),
        22: (sib, (1, 1), None, 16 - NX, 16),
        23: (zp, (0, 0), (0, 3), 8, 16),
        24: (zm, (0, 0), (0, 1), 0, 8),
        25: (zp, (1, 3), (1, 2), 0, NQ),
        26: (zm, (1, 1), (1, 2), 16 - NQ, 16),
        27: (sib, (1, 2), None, 0, NQ),
        28: (sib, (1, 2), None, 16 - NQ, 16),
    }
    left = {ch: set(G) for ch in range(CH)}
    r_left = {ch: set(range(23)) for ch in range(CH)}

    def g_send(ch, *ks):
        for k in ks:
            to, sent, _, lo, hi = G[k]
            g_copy(ch, k, to, block(*sent), lo, hi).start()

    def g_recv(ch, *ks):
        for k in ks:
            to, sent, got, lo, hi = G[k]
            blk = block(*sent, core=other) if got is None else block(*got)
            g_copy(ch, k, to, blk, lo, hi).wait_recv()

    def g_sent(ch, *ks):
        for k in ks:
            left[ch].remove(k)
            to, sent, _, lo, hi = G[k]
            g_copy(ch, k, to, block(*sent), lo, hi).wait_send()

    def g_first(ch):
        g_send(ch, 0, 1, 2, 3)

    def g_own(ch):
        g_sent(ch, 0, 1)
        g_send(ch, 23, 24)

    def g_second(ch):
        g_recv(ch, 0)
        g_send(ch, 4, 19)
        g_recv(ch, 1)
        g_send(ch, 6, 20)

    def g_third(ch):
        g_recv(ch, 2)
        g_sent(ch, 4, 6)
        g_send(ch, 8, 9, 10)

    def g_fourth(ch):
        g_recv(ch, 4)
        g_send(ch, 11, 13)
        g_recv(ch, 6)
        g_send(ch, 12, 14)

    def g_fifth(ch):
        g_recv(ch, 19)
        g_send(ch, 25, 21)
        g_recv(ch, 20)
        g_send(ch, 26, 22)
        g_recv(ch, 23)
        g_send(ch, 5)
        g_recv(ch, 24)
        g_send(ch, 7)

    def g_sixth(ch):
        g_recv(ch, 8)
        g_send(ch, 15)
        g_recv(ch, 9)
        g_send(ch, 16)

    def g_last(ch):
        g_recv(ch, 11)
        g_send(ch, 17)
        g_recv(ch, 12)
        g_send(ch, 18)
        g_recv(ch, 25)
        g_send(ch, 27)
        g_recv(ch, 26)
        g_send(ch, 28)
        g_recv(ch, 3, 5, 7, 10, 13, 14, 15, 16, 21, 22, 17, 18, 27, 28)

    def at_y(d):
        return (y + d) % 4

    alo, ahi = pl.ds(0, HA), pl.ds(HA, HA)
    blo, bhi = pl.ds(NA, HB), pl.ds(NA + HB, HB)
    zlo, zhi = pl.ds(0, HB), pl.ds(HB, HB)
    sides = (1 - l, l)

    def r_copy(ch, k):
        o = outs[ch]
        if k < 4:
            src, dst, to = o.at[at_y(k) * 2 + (1 - l), pl.ds(0, NA)], rxa[ch].at[k], xl
        elif k < 16:
            q = (k - 4) // 6
            where, part, dst, to = {
                0: (at_y(2), blo, rb1l[ch].at[q], ym),
                1: (at_y(2), bhi, rb1h[ch].at[q], yp),
                2: (at_y(1), blo, rbm[ch].at[q, zlo], yp),
                3: (at_y(3), bhi, rbp[ch].at[q, zhi], ym),
                4: (at_y(3), blo, rbp[ch].at[q, zlo], ym),
                5: (at_y(1), bhi, rbm[ch].at[q, zhi], yp),
            }[(k - 4) % 6]
            src = o.at[where * 2 + sides[q], part]
        elif k < 22:
            where, part, dst, to = {
                16: (at_y(2), alo, ra1l[ch], ym),
                17: (at_y(2), ahi, ra1h[ch], yp),
                18: (at_y(1), alo, ram[ch].at[alo], yp),
                19: (at_y(3), ahi, rap[ch].at[ahi], ym),
                20: (at_y(3), alo, rap[ch].at[alo], ym),
                21: (at_y(1), ahi, ram[ch].at[ahi], yp),
            }[k]
            src = o.at[where * 2 + l, part]
        else:
            src, dst, to = sxb[ch], rxb[ch], xl
        return pltpu.make_async_remote_copy(
            src, dst, rs.at[ch, k], rr.at[ch, k], device_id=to, device_id_type=MESH
        )

    def r_send(ch, *ks):
        for k in ks:
            r_copy(ch, k).start()

    def r_recv(ch, *ks):
        for k in ks:
            r_copy(ch, k).wait_recv()

    def r_sent(ch, *ks):
        for k in ks:
            r_left[ch].remove(k)
            r_copy(ch, k).wait_send()

    def add_to(ch, part, at, count, got):
        o = outs[ch]
        for t in range(count):
            o[part, at + t] = (o[part, at + t].astype(F32) + got[t].astype(F32)).astype(BF16)

    def r_first(ch):
        r_send(ch, 4, 5, 2, 6, 7)

    def r_second(ch):
        r_sent(ch, 4, 5, 2)
        r_send(ch, 10, 11, 1, 3)

    def r_third(ch):
        r_recv(ch, 4)
        add_to(ch, at_y(3) * 2 + sides[0], NA, HB, rb1l[ch].at[0])
        r_send(ch, 8)
        r_recv(ch, 5)
        add_to(ch, at_y(1) * 2 + sides[0], NA + HB, HB, rb1h[ch].at[0])
        r_send(ch, 9)
        r_recv(ch, 2)
        add_to(ch, at_y(2) * 2 + l, 0, NA, rxa[ch].at[2])
        r_send(ch, 16, 17, 0)

    def r_fourth(ch):
        r_recv(ch, 10)
        add_to(ch, at_y(3) * 2 + sides[1], NA, HB, rb1l[ch].at[1])
        r_send(ch, 14)
        r_recv(ch, 11)
        add_to(ch, at_y(1) * 2 + sides[1], NA + HB, HB, rb1h[ch].at[1])
        r_send(ch, 15, 12, 13)

    def r_fifth(ch):
        r_recv(ch, 6, 7, 8, 9)
        for t in range(NB):
            total = outs[ch][y * 2 + sides[0], NA + t].astype(F32)
            total = total + rbm[ch][0, t].astype(F32) + rbp[ch][0, t].astype(F32)
            sxb[ch][t] = total.astype(BF16)
        r_send(ch, 22)

    def r_sixth(ch):
        r_recv(ch, 1)
        add_to(ch, at_y(1) * 2 + l, 0, NA, rxa[ch].at[1])
        r_send(ch, 18)
        r_recv(ch, 3)
        add_to(ch, at_y(3) * 2 + l, 0, NA, rxa[ch].at[3])
        r_send(ch, 19)

    def r_seventh(ch):
        r_recv(ch, 16)
        add_to(ch, at_y(3) * 2 + l, 0, HA, ra1l[ch])
        r_send(ch, 20)
        r_recv(ch, 17)
        add_to(ch, at_y(1) * 2 + l, HA, HA, ra1h[ch])
        r_send(ch, 21)

    def finish(ch, t, total):
        agg[t, FOF[ch] : FOF[ch] + FCS[ch], :] = (total * lax.rsqrt(deg_ref[t : t + 1, :].astype(F32))).astype(BF16)

    def r_last(ch):
        r_recv(ch, 0, 18, 19, 20, 21)
        for t in range(NA):
            total = outs[ch][y * 2 + l, t].astype(F32) + rxa[ch][0, t].astype(F32)
            finish(ch, t, total + ram[ch][t].astype(F32) + rap[ch][t].astype(F32))
        r_recv(ch, 12, 13, 14, 15, 22)
        for t in range(NB):
            total = outs[ch][y * 2 + l, NA + t].astype(F32) + rxb[ch][t].astype(F32)
            finish(ch, NA + t, total + rbm[ch][1, t].astype(F32) + rbp[ch][1, t].astype(F32))

    def products(ch, events):
        x = xs[ch]

        def body(i, acc):
            for at, act in events:
                pl.when(i == at)(act)
            for u in range(UNROLL):
                spot = (i % 2) * (2 * UNROLL) + 2 * u
                first = jnp.clip(plan_s[i // 2, spot], 0, SLOTS * 256 + 255)
                second = jnp.clip(plan_s[i // 2, spot + 1], 0, SLOTS * 256 + 255)
                keep = plan_s[ROW_KEEP + i // 4, (i % 4) * UNROLL + u].astype(F32)
                values = jnp.concatenate([a_buf[first >> 8], a_buf[second >> 8]], axis=1)
                nodes = jnp.concatenate([x[first & 255], x[second & 255]], axis=1)
                acc = acc * keep + lax.dot_general(nodes, values, NT, preferred_element_type=F32)
                s_buf[i * UNROLL + u, 0 : FCS[ch]] = acc.astype(BF16)
            return acc

        lax.fori_loop(0, ITERS, body, jnp.zeros((FCS[ch], T), F32))

    def extract(ch):
        o = outs[ch]

        def body(i, _):
            for u in range(16):
                o[i, u] = s_buf[jnp.clip(plan_s[ROW_END, i * 16 + u], 0, STEPS), 0 : FCS[ch]]
            return 0

        lax.fori_loop(0, 8, body, 0)

    g_first(0)
    g_own(0)
    make_plan(rows_ref, cols_ref, live_ref[0], plan_v)
    to_smem = pltpu.make_async_copy(plan_v, plan_s, p_sem)
    to_smem.start()
    g_second(0)
    g_third(0)
    g_fourth(0)
    g_fifth(0)
    g_first(1)
    g_send(1, 23, 24)
    to_smem.wait()
    for load in loads:
        load.wait()
    g_sixth(0)
    g_last(0)

    products(
        0,
        [
            (4, lambda: g_second(1)),
            (7, lambda: g_third(1)),
            (9, lambda: g_fourth(1)),
            (10, lambda: g_fifth(1)),
            (12, lambda: g_sixth(1)),
        ],
    )
    extract(0)
    r_first(0)
    g_last(1)
    products(
        1,
        [
            (1, lambda: r_second(0)),
            (3, lambda: r_third(0)),
            (6, lambda: r_fourth(0)),
            (9, lambda: r_fifth(0)),
            (10, lambda: r_sixth(0)),
            (12, lambda: r_seventh(0)),
        ],
    )
    extract(1)
    r_first(1)
    r_second(1)
    r_last(0)
    r_third(1)
    r_fourth(1)
    r_fifth(1)
    r_sixth(1)
    r_seventh(1)
    r_last(1)

    def body(i, _):
        for u in range(4):
            t = i * 4 + u
            mixed = lax.dot_general(agg[t], weight_ref[...], TN, preferred_element_type=F32)
            out_ref[pl.ds(t * T, T), :] = jnp.maximum(mixed + bias_ref[...], 0.0).astype(BF16)
        return 0

    lax.fori_loop(0, 4, body, 0)
    for ch in range(CH):
        g_sent(ch, *sorted(left[ch]))
        r_sent(ch, *sorted(r_left[ch]))


def per_device(features, degrees, tile_values, tile_rows, tile_cols, tile_live, weight, bias):
    vmem = pl.BlockSpec(memory_space=pltpu.VMEM)
    landing = [(4, NA), (2, HB), (2, HB), (2, NB), (2, NB), (HA,), (HA,), (NA,), (NA,), (NB,), (NB,)]
    return pl.pallas_call(
        kernel,
        out_shape=jax.ShapeDtypeStruct(features.shape, BF16),
        in_specs=[
            vmem, vmem, pl.BlockSpec(memory_space=pl.ANY), vmem, vmem,
            pl.BlockSpec(memory_space=pltpu.SMEM), vmem, vmem,
        ],
        out_specs=vmem,
        scratch_shapes=[
            pltpu.VMEM((SLOTS + 1, T, T), BF16),
            pltpu.VMEM((256, FCS[0], T), BF16),
            pltpu.VMEM((256, FCS[1], T), BF16),
            pltpu.VMEM((STEPS + 1, max(FCS), T), BF16),
            pltpu.VMEM((8, 16, FCS[0], T), BF16),
            pltpu.VMEM((8, 16, FCS[1], T), BF16),
            pltpu.VMEM((16, T), I32),
            pltpu.SMEM((16, T), I32),
            pltpu.VMEM((16, 128, T), BF16),
            *[pltpu.VMEM(shape + (fc, T), BF16) for fc in FCS for shape in landing],
            pltpu.SemaphoreType.DMA((6,)),
            pltpu.SemaphoreType.DMA,
            pltpu.SemaphoreType.DMA((CH, 29)),
            pltpu.SemaphoreType.DMA((CH, 29)),
            pltpu.SemaphoreType.DMA((CH, 23)),
            pltpu.SemaphoreType.DMA((CH, 23)),
        ],
        compiler_params=pltpu.CompilerParams(
            collective_id=0, has_side_effects=True, vmem_limit_bytes=60 << 20
        ),
        name="graph_layer",
    )(
        features,
        degrees.reshape(16, T),
        tile_values,
        tile_rows.reshape(SLOTS // T, T),
        tile_cols.reshape(SLOTS // T, T),
        tile_live,
        weight,
        bias.reshape(1, 128),
    )


def solution(mesh):
    return jax.shard_map(
        per_device,
        mesh=mesh,
        in_specs=(
            P(("rep", "row"), None),
            P(("rep", "row")),
            P(("rep", "row"), None, None),
            P(("rep", "row")),
            P(("rep", "row")),
            P(("rep", "row")),
            P(),
            P(),
        ),
        out_specs=P(("rep", "row"), None),
        check_vma=False,
    )
```

time: 91.4 us -> 79.2 us (0.87)
  Pallas kernels: 88.7 us -> 76.5 us
    pallas_call x1, Pallas kernels: 88.7 us -> 76.5 us  [per_device(): pl.pallas_call(kernel, out_shape=jax.ShapeDtypeStruct(features.shape, BF1...]
where the time goes in v2:
time: 79.2 us; the launch traced here: 79 us
  Pallas kernels  76.5 us (97%)
  local copies, waits for them, and re-layouts  1.87 us (2%)
    pallas_call x1, Pallas kernels, per_device(): pl.pallas_call(kernel, out_shape=jax.ShapeDtypeStruct(features.shape, BF1...  76.5 us
    unnamed x1, local copies, waits for them, and re-layouts  1.87 us

profile of v2, /device:TPU:0, one launch (start us, length us, event | category | flops | bytes accessed | tf_op | source)
XLA Modules:
  0.0 79.0 jit_solution(6751451920638252704)
XLA Ops:
  0.7 76.5 %graph_layer.1 = bf16[2048,128]{1,0:T(8,128)(2,1)} custom-call(bf16[2048,128]{1,0:T(8,128)(2,1)} %feat_ref.1, s32[16,128]{1,0:T(8,128)} %bitcast.4, bf16[768,128,128]{2,1,0:T(8,128)(2,1)} %tiles_ref.1, s32[6,128]{1,0:T(8,128)} %bitcast.5, s32[6,128]{1,0:T(8,128)} %bitcast.6, s32[1]{0:T(128)S(6)} %copy.10.live_ref, bf16[128,128]{1,0:T(8,128)(2,1)} %weight_ref.1, ...), custom_call_target="tpu_custom_call" | custom-call | tf_op jit(solution)/shard_map/graph_layer/pallas_call | solution.py:448
  77.1 1.9 %copy.11 = bf16[2048,128]{1,0:T(8,128)(2,1)} copy(bf16[2048,128]{1,0:T(8,128)(2,1)} %graph_layer.1) | data formatting | bytes 1048576

commit v3 on v2

--- a/solution.py
+++ b/solution.py
@@ -10,21 +10,19 @@
 MESH = pl.DeviceIdType.MESH
 F32, BF16, I32 = jnp.float32, jnp.bfloat16, jnp.int32
 NT = (((1,), (1,)), ((), ()))
-TN = (((0,), (0,)), ((), ()))
 
 T = 128
 CH = 2
-FCS = (64, 64)
-FOF = (0, FCS[0])
+FC = 128 // CH
 SLOTS = 768
 STEPS = 448
-UNROLL = 32
+UNROLL = 64
 ITERS = STEPS // UNROLL
 NX = 6
 NQ = 4
-NA = 6
+NA = 7
 NB = 16 - NA
-HA, HB = NA // 2, NB // 2
+HAL, HAH, HBL, HBH = 3, 4, 5, 4
 ROW_KEEP, ROW_END = 8, 12
 
 
@@ -74,8 +72,8 @@
 
 
 def kernel(
-    feat_ref, deg_ref, tiles_ref, rows_ref, cols_ref, live_ref, weight_ref, bias_ref, out_ref,
-    a_buf, x0, x1, s_buf, o0, o1, plan_v, plan_s, agg,
+    feat_ref, deg_ref, tiles_ref, rows_ref, cols_ref, live_ref, agg,
+    a_buf, x0, x1, s_buf, o0, o1, plan_v, plan_s, scales,
     *rest,
 ):
     bufs, (a_sem, p_sem, gs, gr, rs, rr) = rest[:-6], rest[-6:]
@@ -110,9 +108,14 @@
         turned = feat_ref[t * T : (t + 1) * T, :].T.astype(F32)
         scaled = (turned * scale[t : t + 1, :]).astype(BF16)
         for ch in range(CH):
-            xs[ch][row * 16 + t] = scaled[FOF[ch] : FOF[ch] + FCS[ch], :]
+            xs[ch][row * 16 + t] = scaled[ch * FC : (ch + 1) * FC, :]
+    columns = jnp.concatenate([scale] * 8, axis=0).T
+    for t in range(0, 16, 2):
+        pair = [jnp.broadcast_to(columns[:, t + side : t + side + 1], (T, FC)) for side in range(2)]
+        pair = jnp.concatenate(pair, axis=1)
+        scales[t], scales[t + 1] = pair[: T // 2], pair[T // 2 :]
     a_buf[SLOTS] = jnp.zeros((T, T), BF16)
-    s_buf[STEPS] = jnp.zeros((max(FCS), T), BF16)
+    s_buf[STEPS] = jnp.zeros((T, FC), BF16)
 
     pl.semaphore_wait(barrier, len(partners))
 
@@ -231,9 +234,9 @@
     def at_y(d):
         return (y + d) % 4
 
-    alo, ahi = pl.ds(0, HA), pl.ds(HA, HA)
-    blo, bhi = pl.ds(NA, HB), pl.ds(NA + HB, HB)
-    zlo, zhi = pl.ds(0, HB), pl.ds(HB, HB)
+    alo, ahi = pl.ds(0, HAL), pl.ds(HAL, HAH)
+    blo, bhi = pl.ds(NA, HBL), pl.ds(NA + HBL, HBH)
+    zlo, zhi = pl.ds(0, HBL), pl.ds(HBL, HBH)
     sides = (1 - l, l)
 
     def r_copy(ch, k):
@@ -294,10 +297,10 @@
 
     def r_third(ch):
         r_recv(ch, 4)
-        add_to(ch, at_y(3) * 2 + sides[0], NA, HB, rb1l[ch].at[0])
+        add_to(ch, at_y(3) * 2 + sides[0], NA, HBL, rb1l[ch].at[0])
         r_send(ch, 8)
         r_recv(ch, 5)
-        add_to(ch, at_y(1) * 2 + sides[0], NA + HB, HB, rb1h[ch].at[0])
+        add_to(ch, at_y(1) * 2 + sides[0], NA + HBL, HBH, rb1h[ch].at[0])
         r_send(ch, 9)
         r_recv(ch, 2)
         add_to(ch, at_y(2) * 2 + l, 0, NA, rxa[ch].at[2])
@@ -305,10 +308,10 @@
 
     def r_fourth(ch):
         r_recv(ch, 10)
-        add_to(ch, at_y(3) * 2 + sides[1], NA, HB, rb1l[ch].at[1])
+        add_to(ch, at_y(3) * 2 + sides[1], NA, HBL, rb1l[ch].at[1])
         r_send(ch, 14)
         r_recv(ch, 11)
-        add_to(ch, at_y(1) * 2 + sides[1], NA + HB, HB, rb1h[ch].at[1])
+        add_to(ch, at_y(1) * 2 + sides[1], NA + HBL, HBH, rb1h[ch].at[1])
         r_send(ch, 15, 12, 13)
 
     def r_fifth(ch):
@@ -329,14 +332,17 @@
 
     def r_seventh(ch):
         r_recv(ch, 16)
-        add_to(ch, at_y(3) * 2 + l, 0, HA, ra1l[ch])
+        add_to(ch, at_y(3) * 2 + l, 0, HAL, ra1l[ch])
         r_send(ch, 20)
         r_recv(ch, 17)
-        add_to(ch, at_y(1) * 2 + l, HA, HA, ra1h[ch])
+        add_to(ch, at_y(1) * 2 + l, HAL, HAH, ra1h[ch])
         r_send(ch, 21)
 
     def finish(ch, t, total):
-        agg[t, FOF[ch] : FOF[ch] + FCS[ch], :] = (total * lax.rsqrt(deg_ref[t : t + 1, :].astype(F32))).astype(BF16)
+        rows, at = pl.ds((t % 2) * (T // 2), T // 2), t - t % 2
+        done = (total * scales[t]).astype(BF16)
+        agg[at, rows, ch * FC : (ch + 1) * FC] = done[:, :FC]
+        agg[at + 1, rows, ch * FC : (ch + 1) * FC] = done[:, FC:]
 
     def r_last(ch):
         r_recv(ch, 0, 18, 19, 20, 21)
@@ -355,24 +361,27 @@
             for at, act in events:
                 pl.when(i == at)(act)
             for u in range(UNROLL):
-                spot = (i % 2) * (2 * UNROLL) + 2 * u
-                first = jnp.clip(plan_s[i // 2, spot], 0, SLOTS * 256 + 255)
-                second = jnp.clip(plan_s[i // 2, spot + 1], 0, SLOTS * 256 + 255)
-                keep = plan_s[ROW_KEEP + i // 4, (i % 4) * UNROLL + u].astype(F32)
+                a_row = 64 // UNROLL
+                spot = (i % a_row) * (2 * UNROLL) + 2 * u
+                first = jnp.clip(plan_s[i // a_row, spot], 0, SLOTS * 256 + 255)
+                second = jnp.clip(plan_s[i // a_row, spot + 1], 0, SLOTS * 256 + 255)
+                keep = plan_s[ROW_KEEP + i // (2 * a_row), (i % (2 * a_row)) * UNROLL + u].astype(F32)
                 values = jnp.concatenate([a_buf[first >> 8], a_buf[second >> 8]], axis=1)
                 nodes = jnp.concatenate([x[first & 255], x[second & 255]], axis=1)
-                acc = acc * keep + lax.dot_general(nodes, values, NT, preferred_element_type=F32)
-                s_buf[i * UNROLL + u, 0 : FCS[ch]] = acc.astype(BF16)
+                acc = acc * keep + lax.dot_general(values, nodes, NT, preferred_element_type=F32)
+                s_buf[i * UNROLL + u] = acc.astype(BF16)
             return acc
 
-        lax.fori_loop(0, ITERS, body, jnp.zeros((FCS[ch], T), F32))
+        lax.fori_loop(0, ITERS, body, jnp.zeros((T, FC), F32))
 
     def extract(ch):
         o = outs[ch]
 
         def body(i, _):
-            for u in range(16):
-                o[i, u] = s_buf[jnp.clip(plan_s[ROW_END, i * 16 + u], 0, STEPS), 0 : FCS[ch]]
+            for u in range(0, 16, 2):
+                ends = [jnp.clip(plan_s[ROW_END, i * 16 + u + side], 0, STEPS) for side in range(2)]
+                pair = jnp.concatenate([s_buf[ends[0]], s_buf[ends[1]]], axis=1)
+                o[i, u], o[i, u + 1] = pair[: T // 2], pair[T // 2 :]
             return 0
 
         lax.fori_loop(0, 8, body, 0)
@@ -397,11 +406,11 @@
     products(
         0,
         [
-            (4, lambda: g_second(1)),
-            (7, lambda: g_third(1)),
-            (9, lambda: g_fourth(1)),
-            (10, lambda: g_fifth(1)),
-            (12, lambda: g_sixth(1)),
+            (2, lambda: g_second(1)),
+            (4, lambda: g_third(1)),
+            (5, lambda: g_fourth(1)),
+            (5, lambda: g_fifth(1)),
+            (6, lambda: g_sixth(1)),
         ],
     )
     extract(0)
@@ -410,12 +419,12 @@
     products(
         1,
         [
-            (1, lambda: r_second(0)),
-            (3, lambda: r_third(0)),
-            (6, lambda: r_fourth(0)),
-            (9, lambda: r_fifth(0)),
-            (10, lambda: r_sixth(0)),
-            (12, lambda: r_seventh(0)),
+            (0, lambda: r_second(0)),
+            (2, lambda: r_third(0)),
+            (3, lambda: r_fourth(0)),
+            (5, lambda: r_fifth(0)),
+            (5, lambda: r_sixth(0)),
+            (6, lambda: r_seventh(0)),
         ],
     )
     extract(1)
@@ -429,14 +438,6 @@
     r_seventh(1)
     r_last(1)
 
-    def body(i, _):
-        for u in range(4):
-            t = i * 4 + u
-            mixed = lax.dot_general(agg[t], weight_ref[...], TN, preferred_element_type=F32)
-            out_ref[pl.ds(t * T, T), :] = jnp.maximum(mixed + bias_ref[...], 0.0).astype(BF16)
-        return 0
-
-    lax.fori_loop(0, 4, body, 0)
     for ch in range(CH):
         g_sent(ch, *sorted(left[ch]))
         r_sent(ch, *sorted(r_left[ch]))
@@ -444,26 +445,27 @@
 
 def per_device(features, degrees, tile_values, tile_rows, tile_cols, tile_live, weight, bias):
     vmem = pl.BlockSpec(memory_space=pltpu.VMEM)
-    landing = [(4, NA), (2, HB), (2, HB), (2, NB), (2, NB), (HA,), (HA,), (NA,), (NA,), (NB,), (NB,)]
-    return pl.pallas_call(
+    half = (T // 2, T)
+    landing = [(4, NA), (2, HBL), (2, HBH), (2, NB), (2, NB), (HAL,), (HAH,), (NA,), (NA,), (NB,), (NB,)]
+    aggregated = pl.pallas_call(
         kernel,
-        out_shape=jax.ShapeDtypeStruct(features.shape, BF16),
+        out_shape=jax.ShapeDtypeStruct((16, T, 128), BF16),
         in_specs=[
             vmem, vmem, pl.BlockSpec(memory_space=pl.ANY), vmem, vmem,
-            pl.BlockSpec(memory_space=pltpu.SMEM), vmem, vmem,
+            pl.BlockSpec(memory_space=pltpu.SMEM),
         ],
         out_specs=vmem,
         scratch_shapes=[
             pltpu.VMEM((SLOTS + 1, T, T), BF16),
-            pltpu.VMEM((256, FCS[0], T), BF16),
-            pltpu.VMEM((256, FCS[1], T), BF16),
-            pltpu.VMEM((STEPS + 1, max(FCS), T), BF16),
-            pltpu.VMEM((8, 16, FCS[0], T), BF16),
-            pltpu.VMEM((8, 16, FCS[1], T), BF16),
+            pltpu.VMEM((256, FC, T), BF16),
+            pltpu.VMEM((256, FC, T), BF16),
+            pltpu.VMEM((STEPS + 1, T, FC), BF16),
+            pltpu.VMEM((8, 16) + half, BF16),
+            pltpu.VMEM((8, 16) + half, BF16),
             pltpu.VMEM((16, T), I32),
             pltpu.SMEM((16, T), I32),
-            pltpu.VMEM((16, 128, T), BF16),
-            *[pltpu.VMEM(shape + (fc, T), BF16) for fc in FCS for shape in landing],
+            pltpu.VMEM((16,) + half, F32),
+            *[pltpu.VMEM(shape + half, BF16) for _ in range(CH) for shape in landing],
             pltpu.SemaphoreType.DMA((6,)),
             pltpu.SemaphoreType.DMA,
             pltpu.SemaphoreType.DMA((CH, 29)),
@@ -482,9 +484,9 @@
         tile_rows.reshape(SLOTS // T, T),
         tile_cols.reshape(SLOTS // T, T),
         tile_live,
-        weight,
-        bias.reshape(1, 128),
     )
+    mixed = jnp.dot(aggregated.reshape(features.shape), weight, preferred_element_type=F32)
+    return jnp.maximum(mixed + bias[None, :], 0.0).astype(BF16)
 
 
 def solution(mesh):

time: 79.2 us -> 76.1 us (0.961)
  Pallas kernels: 76.5 us -> 73 us
  matrix products: 0 us -> 2.12 us
  local copies, waits for them, and re-layouts: 1.87 us -> 0.01 us
    pallas_call x1, Pallas kernels: 76.5 us -> 73 us  [per_device(): pl.pallas_call(kernel, out_shape=jax.ShapeDtypeStruct((16, T, 128), BF16)...]
    dot_general x0 -> x1, matrix products: none -> 2.12 us  [per_device(): jnp.dot(aggregated.reshape(features.shape), weight, preferred_element_typ...]
    unnamed x1 -> x4, local copies, waits for them, and re-layouts: 1.87 us -> 0.01 us
where the time goes in v3:
time: 76.1 us; the launch traced here: 75.8 us
  Pallas kernels  73 us (96%)
  matrix products  2.12 us (3%)
    pallas_call x1, Pallas kernels, per_device(): pl.pallas_call(kernel, out_shape=jax.ShapeDtypeStruct((16, T, 128), BF16)...  73 us
    dot_general x1, matrix products, per_device(): jnp.dot(aggregated.reshape(features.shape), weight, preferred_element_typ...  2.12 us

profile of v3, /device:TPU:0, one launch (start us, length us, event | category | flops | bytes accessed | tf_op | source)
XLA Modules:
  0.0 75.8 jit_solution(612143078902784974)
XLA Ops:
  0.0 0.0 copy-start
  0.0 0.0 copy-start.1
  0.7 73.0 %graph_layer.1 = bf16[16,128,128]{2,1,0:T(8,128)(2,1)} custom-call(bf16[2048,128]{1,0:T(8,128)(2,1)} %feat_ref.1, s32[16,128]{1,0:T(8,128)} %bitcast.7, bf16[768,128,128]{2,1,0:T(8,128)(2,1)} %tiles_ref.1, s32[6,128]{1,0:T(8,128)} %bitcast.8, s32[6,128]{1,0:T(8,128)} %bitcast.9, s32[1]{0:T(128)S(6)} %copy.9.live_ref), custom_call_target="tpu_custom_call" | custom-call | tf_op jit(solution)/shard_map/graph_layer/pallas_call | solution.py:450
  73.7 0.0 copy-done
  73.7 0.0 copy-done.1
  73.7 2.1 %fusion.1 = bf16[2048,128]{1,0:T(8,128)(2,1)} fusion(bf16[2048,128]{1,0:T(8,128)(2,1)} %bitcast.6, bf16[128,128]{1,0:T(8,128)(2,1)S(1)} %copy-done, f32[128]{0:T(128)S(1)} %copy-done.1), kind=kOutput, calls=%fused_computation.2 | convolution fusion | flops 67895296 | bytes 1081856 | tf_op jit(solution)/shard_map/dot_general | solution.py:488
Async XLA Ops:
  0.0 73.7 %copy-start = (bf16[128,128]{1,0:T(8,128)(2,1)S(1)}, bf16[128,128]{1,0:T(8,128)(2,1)}, u32[]{:S(2)}) copy-start(bf16[128,128]{1,0:T(8,128)(2,1)} %param.14) | copy-start | bytes 98308
  0.0 73.7 %copy-start.1 = (f32[128]{0:T(128)S(1)}, f32[128]{0:T(128)}, u32[]{:S(2)}) copy-start(f32[128]{0:T(128)} %param.15) | copy-start | bytes 1540
